TPU v7x, 128 devices: a whole 4x4x4 slice. The times are simulated.
128 devices in a mesh: seq: 16 (over y, z_hi, core), tensor: 8 (over z_lo, x).
Axes of the slice: x: 4, y: 4, z: 4 (z_hi: 2, z_lo: 2; z = z_hi * 2 + z_lo), core: 2. Of those that a mesh axis runs over, the one named last changes fastest.
Arguments:
- queries: bfloat16 [2048, 4096], P('seq', 'tensor'), may hold values from -32 to 32
- key_rows: bfloat16 [2048, 1024], P('seq', 'tensor'), may hold values from -32 to 32
- values: bfloat16 [2048, 1024], P('seq', 'tensor'), may hold values from -6 to 6
- out_weight: bfloat16 [4096, 8192], P('tensor'), may hold values from -0.09375 to 0.09375
- out_grad: bfloat16 [2048, 8192], P(('seq', 'tensor')), may hold values from -6 to 6
- doc_lengths: int32 [12], replicated, may hold values from 1 to 1024, 2048 in all
Outputs:
- projected: bfloat16 [2048, 8192], P(('seq', 'tensor'))
- query_grad: bfloat16 [2048, 4096], P('seq', 'tensor')
- key_grad: bfloat16 [2048, 1024], P('seq', 'tensor')
- value_grad: bfloat16 [2048, 1024], P('seq', 'tensor')
Inputs may be any that keep to these rules, and one draw needn't show every extreme that they name: `doc_lengths`: 12 document lengths, each 1 or more, summing to 2048; the longest is exactly 1024.
All inputs are finite; a program needn't handle non-finite values.
Results may differ from a plain program's by a relative error of at most 0.03.
Values may be sent and summed in bfloat16 or wider, within the bound.
A program may use at most 64 MiB of HBM per device.

v0:
```python
import math

import jax
import jax.numpy as jnp
from jax import lax
from jax.sharding import PartitionSpec as P

QHEADS = 32
KVHEADS = 8
HEAD = 128


def doc_index(doc_lengths, token_total):
    doc_ends = jnp.cumsum(doc_lengths)
    positions = jnp.arange(token_total, dtype=jnp.int32)
    return jnp.sum((doc_ends[:, None] <= positions[None, :]).astype(jnp.int32), axis=0)


def allowed_pairs(query_docs, query_pos, key_docs, key_pos):
    return (query_docs[:, None] == key_docs[None, :]) & (key_pos[None, :] <= query_pos[:, None])


def head_scores(query_four, key_flat):
    key_three = key_flat.reshape(key_flat.shape[0], -1, HEAD)
    return jnp.einsum(
        "tkgd,skd->tkgs", query_four, key_three, preferred_element_type=jnp.float32
    ) * (1.0 / math.sqrt(HEAD))


def score_grads(query_four, grad_four, log_total, row_delta, allowed, key_flat, value_flat):
    scores = head_scores(query_four, key_flat)
    value_three = value_flat.reshape(value_flat.shape[0], -1, HEAD)
    probs = jnp.where(allowed[:, None, None, :], jnp.exp(scores - log_total[..., None]), 0.0)
    slopes = jnp.einsum(
        "tkgd,skd->tkgs", grad_four, value_three, preferred_element_type=jnp.float32
    )
    score_grad = (probs * (slopes - row_delta[..., None]) * (1.0 / math.sqrt(HEAD))).astype(
        jnp.bfloat16
    )
    return (probs, score_grad)


def body(queries, key_rows, values, out_weight, out_grad, doc_lengths):
    row_count = queries.shape[0]
    seq_count = lax.axis_size("seq")
    token_total = row_count * seq_count
    kv_local = key_rows.shape[1] // HEAD
    group_size = QHEADS // KVHEADS
    documents = doc_index(doc_lengths, token_total)
    first_row = lax.axis_index("seq") * row_count
    own_positions = first_row + jnp.arange(row_count, dtype=jnp.int32)
    own_docs = lax.dynamic_slice_in_dim(documents, first_row, row_count)
    query_four = queries.reshape(row_count, kv_local, group_size, HEAD)
    stat_shape = (row_count, kv_local, group_size)
    run_peak = jnp.full(stat_shape, -1e30, jnp.float32)
    key_piece = lax.all_gather(key_rows, "seq", axis=0, tiled=True)
    value_piece = lax.all_gather(values, "seq", axis=0, tiled=True)
    span_rows = key_piece.shape[0]
    key_pos = jnp.arange(span_rows, dtype=jnp.int32)
    allowed = allowed_pairs(own_docs, own_positions, documents, key_pos)[:, None, None, :]
    scores = jnp.where(allowed, head_scores(query_four, key_piece), -1e30)
    new_peak = jnp.maximum(run_peak, jnp.max(scores, axis=-1))
    probs = jnp.where(allowed, jnp.exp(scores - new_peak[..., None]), 0.0)
    value_three = value_piece.reshape(span_rows, kv_local, HEAD).astype(jnp.float32)
    weighted = jnp.einsum(
        "tkgs,skd->tkgd",
        probs,
        value_three,
        precision=lax.Precision.HIGHEST,
        preferred_element_type=jnp.float32,
    )
    run_peak, run_total, weighted = (new_peak, jnp.sum(probs, axis=-1), weighted)
    log_total = run_peak + jnp.log(run_total)
    attn_four = (weighted / run_total[..., None]).astype(jnp.bfloat16)
    attended = attn_four.reshape(row_count, -1)
    projected = lax.psum_scatter(
        jnp.dot(attended, out_weight, preferred_element_type=jnp.float32).astype(jnp.bfloat16),
        "tensor",
        scatter_dimension=0,
        tiled=True,
    )
    attn_grad = lax.dot_general(
        lax.all_gather(out_grad, "tensor", axis=0, tiled=True),
        out_weight,
        (((1,), (1,)), ((), ())),
        preferred_element_type=jnp.float32,
    ).astype(jnp.bfloat16)
    grad_four = attn_grad.reshape(row_count, kv_local, group_size, HEAD)
    row_delta = jnp.sum(grad_four.astype(jnp.float32) * attn_four.astype(jnp.float32), axis=-1)
    all_log, all_delta = (
        lax.all_gather(log_total, "seq", axis=0, tiled=True),
        lax.all_gather(row_delta, "seq", axis=0, tiled=True),
    )
    key_piece = lax.all_gather(key_rows, "seq", axis=0, tiled=True)
    value_piece = lax.all_gather(values, "seq", axis=0, tiled=True)
    query_piece = lax.all_gather(queries, "seq", axis=0, tiled=True)
    grad_piece = lax.all_gather(attn_grad, "seq", axis=0, tiled=True)
    span_rows = key_piece.shape[0]
    piece_pos = jnp.arange(span_rows, dtype=jnp.int32)
    allowed = allowed_pairs(own_docs, own_positions, documents, piece_pos)
    probs, score_grad = score_grads(
        query_four, grad_four, log_total, row_delta, allowed, key_piece, value_piece
    )
    key_three = key_piece.reshape(span_rows, kv_local, HEAD)
    query_grad = jnp.einsum(
        "tkgs,skd->tkgd", score_grad, key_three, preferred_element_type=jnp.float32
    )
    piece_four = query_piece.reshape(span_rows, kv_local, group_size, HEAD)
    grad_piece_four = grad_piece.reshape(span_rows, kv_local, group_size, HEAD)
    reverse_allowed = allowed_pairs(documents, piece_pos, own_docs, own_positions)
    back_probs, back_grad = score_grads(
        piece_four, grad_piece_four, all_log, all_delta, reverse_allowed, key_rows, values
    )
    key_grad = jnp.einsum(
        "tkgs,tkgd->skd", back_grad, piece_four, preferred_element_type=jnp.float32
    )
    value_grad = jnp.einsum(
        "tkgs,tkgd->skd",
        back_probs.astype(jnp.bfloat16),
        grad_piece_four,
        preferred_element_type=jnp.float32,
    )
    query_grad, key_grad, value_grad = (query_grad, key_grad, value_grad)
    return (
        projected,
        query_grad.reshape(row_count, -1).astype(jnp.bfloat16),
        key_grad.reshape(row_count, -1).astype(jnp.bfloat16),
        value_grad.reshape(row_count, -1).astype(jnp.bfloat16),
    )


def solution(mesh):
    placed = (
        P("seq", "tensor"),
        P("seq", "tensor"),
        P("seq", "tensor"),
        P("tensor", None),
        P(("seq", "tensor"), None),
        P(),
    )
    return jax.shard_map(
        body,
        mesh=mesh,
        in_specs=placed,
        out_specs=(
            P(("seq", "tensor"), None),
            P("seq", "tensor"),
            P("seq", "tensor"),
            P("seq", "tensor"),
        ),
        check_vma=False,
    )
```

profile of v0, /device:TPU:0, one launch (start us, length us, event | category | flops | bytes accessed | tf_op | source)
XLA Modules:
  0.0 207.4 jit_solution(15436938414877378987)
XLA Ops:
  7.2 0.0 all-gather.6.cloned.1.call-start
  7.2 0.7 all-gather.6.cloned.1.call-update
  7.9 0.0 all-gather.8.cloned.1.call-start
  7.9 1.7 copy.52
  9.6 0.0 all-gather.8.cloned.1.call-update
  9.7 0.0 all-gather.10.cloned.1.call-start
  9.7 43.8 %all-gather.6.cloned.1.call-done = bf16[128,8192]{1,0:T(8,128)(2,1)} async-done(((bf16[16,8192]{1,0:T(8,128)(2,1)}), bf16[128,8192]{1,0:T(8,128)(2,1)}) %all-gather.6.cloned.1.call-update) | async-done | bytes 2097168 | tf_op jit(solution)/shard_map/all_gather | solution.py:83
  53.5 7.6 %convolution_convert_fusion.1 = bf16[128,512]{1,0:T(8,128)(2,1)} fusion(bf16[128,8192]{1,0:T(8,128)(2,1)} %all-gather.6.cloned.1.call-done, bf16[512,8192]{1,0:T(8,128)(2,1)} %param.9), kind=kOutput, calls=%fused_computation.37 | convolution fusion | flops 1073807360 | bytes 10616832 | tf_op jit(solution)/shard_map/dot_general | solution.py:82
  61.2 0.0 reduce-scatter.2.cloned.1.call-start
  61.2 0.2 reduce-window.8
  61.4 0.1 copy.44
  61.5 0.1 convert_reduce_fusion
  61.6 0.1 dynamic_slice.3
  61.7 25.9 %all_gather.23 = bf16[2048,128]{1,0:T(8,128)(2,1)S(1)} all-gather(bf16[128,128]{1,0:T(8,128)(2,1)S(1)} %copy-done.3), channel_id=1, replica_groups=mesh['seq'=16,'tensor'=8] {'seq'}, dimensions={0}, use_global_device_ids=true | all-gather | bytes 557056 | tf_op jit(solution)/shard_map/all_gather | solution.py:56
  87.6 0.3 fusion.48
  88.0 0.7 fusion.13
  88.7 20.7 %all_gather.24 = bf16[2048,128]{0,1:T(8,128)(2,1)S(1)} all-gather(bf16[128,128]{0,1:T(8,128)(2,1)S(1)} %copy.44), channel_id=1, replica_groups=mesh['seq'=16,'tensor'=8] {'seq'}, dimensions={0}, use_global_device_ids=true | all-gather | bytes 557056 | tf_op jit(solution)/shard_map/all_gather | solution.py:57
  109.4 1.0 fusion.14
  110.5 0.1 copy.49
  110.6 4.6 %multiply_reduce_fusion = (f32[128,4]{0,1:T(4,128)S(1)}, bf16[1,128,128,4]{2,1,3,0:T(8,128)(2,1)S(1)}) fusion(f32[128,1,4,128]{0,3,2,1:T(8,128)S(1)} %bitcast.238, f32[128,4]{0,1:T(4,128)S(1)} %fusion.14, bf16[2048,128]{0,1:T(8,128)(2,1)S(1)} %all_gather.24, f32[2048,128,4]{1,0,2:T(8,128)} %copy-done, f32[128,4]{0,1:T(4,128)S(1)} %broadcast_maximum_fusion, ...), kind=kOutput, calls=%fused_computation.54 | convolution fusion | flops 1615134208 | bytes 5380096 | tf_op jit(solution)/shard_map/tkgs,skd->tkgd/dot_general | solution.py:65
  115.2 6.1 %convolution_convert_fusion = bf16[128,8192]{1,0:T(8,128)(2,1)} fusion(bf16[128,512]{0,1:T(8,128)(2,1)S(1)} %bitcast.240, bf16[512,8192]{1,0:T(8,128)(2,1)} %param.9), kind=kOutput, calls=%fused_computation | convolution fusion | flops 1074790400 | bytes 10616832 | tf_op jit(solution)/shard_map/dot_general | solution.py:77
  121.4 23.0 %all-gather = f32[2048,4]{0,1:T(4,128)S(1)} all-gather(f32[128,4]{0,1:T(4,128)S(1)} %log_add_fusion), channel_id=2, replica_groups=mesh['seq'=16,'tensor'=8] {'seq'}, dimensions={0}, use_global_device_ids=true | all-gather | bytes 34816 | tf_op jit(solution)/shard_map/all_gather | solution.py:91
  144.4 0.4 fusion.49
  144.8 3.9 %fusion.30 = bf16[128,4,128]{0,2,1:T(8,128)(2,1)S(1)} fusion(f32[2048,128,4]{1,0,2:T(8,128)} %copy-done, f32[128,4]{0,1:T(4,128)S(1)} %get-tuple-element.18, f32[128,4]{0,1:T(4,128)S(1)} %log_add_fusion, pred[128,2048]{0,1:T(8,128)(4,1)S(1)} %fusion.48, bf16[2048,128]{0,1:T(8,128)(2,1)S(1)} %all_gather.24, bf16[2048,128]{1,0:T(8,128)(2,1)S(1)} %all_gather.23, ...), kind=kOutput, calls=%fused_computation.36 | convolution fusion | flops 544276480 | bytes 5771264 | tf_op jit(solution)/shard_map/tkgs,skd->tkgd/dot_general | solution.py:105
  148.8 0.8 copy.59
  149.5 19.5 %all-gather.1 = f32[2048,4]{0,1:T(4,128)S(1)} all-gather(f32[128,4]{0,1:T(4,128)S(1)} %get-tuple-element.18), channel_id=3, replica_groups=mesh['seq'=16,'tensor'=8] {'seq'}, dimensions={0}, use_global_device_ids=true | all-gather | bytes 34816 | tf_op jit(solution)/shard_map/all_gather | solution.py:92
  169.0 4.9 %bitcast_select_fusion = f32[2048,1,4,128]{0,3,2,1:T(8,128)} fusion(bf16[2048,4,128]{0,2,1:T(8,128)(2,1)} %bitcast.236, f32[2048,4]{0,1:T(4,128)S(1)} %all-gather, pred[2048,128]{0,1:T(8,128)(4,1)S(1)} %fusion.49, bf16[128,128]{1,0:T(8,128)(2,1)S(1)} %copy-done.3), kind=kOutput, calls=%fused_computation.11 | convolution fusion | flops 271581184 | bytes 6619136 | tf_op jit(solution)/shard_map/tkgd,skd->tkgs/dot_general | solution.py:25
  173.9 2.9 %copy.72 = bf16[2048,512]{0,1:T(8,128)(2,1)S(1)} copy(bf16[2048,512]{1,0:T(8,128)(2,1)} %all-gather.10.cloned.1.call-done) | data formatting | bytes 4194304 | tf_op jit(solution)/shard_map/reshape.46
  176.9 2.9 %fusion.39 = bf16[128,128]{0,1:T(8,128)(2,1)S(1)} fusion(bf16[2048,4,128]{0,2,1:T(8,128)(2,1)S(1)} %bitcast.234, f32[2048,1,4,128]{0,3,2,1:T(8,128)} %bitcast_select_fusion), kind=kOutput, calls=%fused_computation.42 | convolution fusion | flops 269500416 | bytes 6324224 | tf_op jit(solution)/shard_map/tkgs,tkgd->skd/dot_general | solution.py:117
  179.8 0.7 copy.60
  180.5 4.9 %fusion.35 = bf16[128,128]{1,0:T(8,128)(2,1)} fusion(bf16[2048,4,128]{0,2,1:T(8,128)(2,1)} %bitcast.237, f32[2048,1,4,128]{0,3,2,1:T(8,128)} %bitcast_select_fusion, bf16[2048,4,128]{0,2,1:T(8,128)(2,1)S(1)} %bitcast.235, f32[2048,4]{0,1:T(4,128)S(1)} %all-gather.1, bf16[128,128]{1,0:T(8,128)(2,1)S(1)} %copy-done.4), kind=kOutput, calls=%fused_computation.40 | convolution fusion | flops 541081600 | bytes 8486912 | tf_op jit(solution)/shard_map/tkgs,tkgd->skd/dot_general | solution.py:114
  185.4 15.4 %reduce-scatter.2.cloned.1.call-done = bf16[16,8192]{1,0:T(8,128)(2,1)} async-done(((bf16[128,8192]{1,0:T(8,128)(2,1)}), bf16[16,8192]{1,0:T(8,128)(2,1)}) %reduce-scatter.2.cloned.1.call-update) | async-done | bytes 262160 | tf_op jit(solution)/shard_map/reduce_scatter | solution.py:76
  (19 shorter events, 0.1 us)
Async XLA Ops:
  7.2 46.3 %all-gather.6.cloned.1.call-start = ((), (), s32[]{:S(2)}) async-start(), calls=%async_computation.2 | async-start | bytes 2359296 | tf_op jit(solution)/shard_map/all_gather | solution.py:83
  7.9 161.1 %all-gather.8.cloned.1.call-start = ((), (), s32[]{:S(2)}) async-start(), calls=%async_computation.3 | async-start | bytes 2228224 | tf_op jit(solution)/shard_map/all_gather | solution.py:96
  9.6 51.6 %copy-start.5 = (s32[12]{0:T(128)S(1)}, s32[12]{0:T(128)}, u32[]{:S(2)}) copy-start(s32[12]{0:T(128)} %param.11) | copy-start | bytes 148
  9.7 51.7 %copy-start.4 = (bf16[128,128]{1,0:T(8,128)(2,1)S(1)}, bf16[128,128]{1,0:T(8,128)(2,1)}, u32[]{:S(2)}) copy-start(bf16[128,128]{1,0:T(8,128)(2,1)} %param.8) | copy-start | bytes 98308
  9.7 52.0 %copy-start.3 = (bf16[128,128]{1,0:T(8,128)(2,1)S(1)}, bf16[128,128]{1,0:T(8,128)(2,1)}, u32[]{:S(2)}) copy-start(bf16[128,128]{1,0:T(8,128)(2,1)} %param.7) | copy-start | bytes 98308
  9.7 78.3 %copy-start.2 = (bf16[128,512]{1,0:T(8,128)(2,1)S(1)}, bf16[128,512]{1,0:T(8,128)(2,1)}, u32[]{:S(2)}) copy-start(bf16[128,512]{1,0:T(8,128)(2,1)} %param.6) | copy-start | bytes 393220
  9.7 164.2 %all-gather.10.cloned.1.call-start = ((), (), s32[]{:S(2)}) async-start(), calls=%async_computation.4 | async-start | bytes 2228224 | tf_op jit(solution)/shard_map/all_gather | solution.py:97
  61.2 139.7 %reduce-scatter.2.cloned.1.call-start = ((), (), s32[]{:S(2)}) async-start(), calls=%async_computation.1 | async-start | bytes 2359296 | tf_op jit(solution)/shard_map/reduce_scatter | solution.py:76
  87.9 22.5 %copy-start.1 = (bf16[128,512]{1,0:T(8,128)(2,1)S(1)}, bf16[128,512]{1,0:T(8,128)(2,1)}, u32[]{:S(2)}) copy-start(bf16[128,512]{1,0:T(8,128)(2,1)} %convolution_convert_fusion.1) | copy-start | bytes 393220
  88.7 20.7 %copy-start = (f32[2048,128,4]{1,0,2:T(8,128)}, f32[2048,128,4]{1,0,2:T(8,128)S(1)}, u32[]{:S(2)}) copy-start(f32[2048,128,4]{1,0,2:T(8,128)S(1)} %get-tuple-element.17) | copy-start | bytes 12582916
Sparse Core Ops, SparseCore 0:
  9.6 43.8 all-gather.5
  55.8 52.1 all-gather.7
  110.4 46.2 all-gather.9
  159.6 41.2 reduce-scatter.1
where the time goes:
time: 208 us; the launch traced here: 207 us
  blocking collectives  89.1 us (43%)
  waiting for transfers between devices  59.9 us (29%)
  matrix products  35.7 us (17%)
  between operations  13.9 us (7%)
  local copies, waits for them, and re-layouts  6.43 us (3%)
  other arithmetic  2.11 us (1%)
    all_gather x1, waiting for transfers between devices, body(): lax.all_gather(out_grad, 'tensor', axis=0, tiled=True)  43.8 us
    all_gather x1, blocking collectives, body(): key_piece = lax.all_gather(key_rows, 'seq', axis=0, tiled=True)  25.9 us
    all_gather x1, blocking collectives, body(): lax.all_gather(log_total, 'seq', axis=0, tiled=True)  23 us
    all_gather x1, blocking collectives, body(): value_piece = lax.all_gather(values, 'seq', axis=0, tiled=True)  20.7 us
    all_gather x1, blocking collectives, body(): lax.all_gather(row_delta, 'seq', axis=0, tiled=True)  19.5 us
    reduce_scatter x1, waiting for transfers between devices, body(): lax.psum_scatter(jnp.dot(attended, out_weight, preferred_element_type=jnp...  15.4 us
    dot_general x1, matrix products, body(): lax.dot_general(lax.all_gather(out_grad, 'tensor', axis=0, tiled=True), o...  7.62 us
    dot_general x1, matrix products, body(): jnp.dot(attended, out_weight, preferred_element_type=jnp.float32)  6.11 us
  transfers between devices with their start and end apart: 4, of which 2 were waited for; matrix products, arithmetic and copies ran while one was open for 21% of the time, Pallas kernels for 0%

commit v1 on v0

v1 whole, which is shorter than its diff:
```python
import math

import jax
import jax.numpy as jnp
from jax import lax
from jax.experimental import pallas as pl
from jax.experimental.pallas import tpu as pltpu
from jax.sharding import PartitionSpec as P

HEAD = 128
GROUP = 4
ROWS = 128
COLS = GROUP * HEAD
D = 8192
DOCS = 12
PART = 16
SLOTS = 9
NA = 4
AW = D // NA
NC = 8
CW = D // NC
SCALE = 1.0 / math.sqrt(HEAD)
MESH = pl.DeviceIdType.MESH
F32 = jnp.float32
BF16 = jnp.bfloat16


def dot(a, b, dims=((1,), (0,))):
    return lax.dot_general(a, b, (dims, ((), ())), preferred_element_type=F32)


def fold(a, op):
    return op(a.reshape(a.shape[0] // 8, 8, a.shape[1]), axis=0)


def kernel(
    docs_ref, q_hbm, k_hbm, v_hbm, w_hbm, g_hbm,
    proj_ref, dq_ref, dk_ref, dv_ref,
    w, g, q, qt, q4, kv, sc, pr, mx, ot, o, oz, zs, rz, tb, rl, xin,
    acc, do, dz, dost, dos4, dsb, dkv, ci, ri,
    lsem, wsem,
    agx_s, agx_r, agz_s, agz_r,
    kv_s, kv_r, kf_s,
    zh_s, zh_r,
    a_s, a_r, rl_s, rl_r, x_s, x_r,
    ci_s, ci_r, ri_s, ri_r,
):
    s, t = lax.axis_index("seq"), lax.axis_index("tensor")
    c, chip = s % 2, s // 2
    zh = chip % 2
    zl, x = t // 4, t % 4
    sz = s + 2 - 4 * zh
    tz = t + 4 - 8 * zl

    def at(seq, tensor):
        return {"seq": seq, "tensor": tensor}

    xr, xl = at(s, zl * 4 + (x + 1) % 4), at(s, zl * 4 + (x + 3) % 4)
    zp, zq, zhp = at(s, tz), at(sz, tz), at(sz, t)
    core = at(s + 1 - 2 * c, t)

    def chip_at(offset):
        return at(((chip + offset) % 8) * 2 + c, t)

    sent = []

    def send(src, dst, ss, rs, dev):
        copy = pltpu.make_async_remote_copy(
            src_ref=src, dst_ref=dst, send_sem=ss, recv_sem=rs, device_id=dev, device_id_type=MESH
        )
        copy.start()
        return copy

    def keep(*args):
        sent.append(send(*args))

    def arrived(dst, rs, dev, ss):
        pltpu.make_async_remote_copy(
            src_ref=dst, dst_ref=dst, send_sem=ss, recv_sem=rs, device_id=dev, device_id_type=MESH
        ).wait_recv()

    def block(pos):
        return pl.ds(pl.multiple_of(pos * PART, PART), PART)

    left, right, opp = (x + 3) % 4, (x + 1) % 4, (x + 2) % 4

    load_k = pltpu.make_async_copy(k_hbm, kv.at[0:ROWS, 0:HEAD], lsem.at[0])
    load_v = pltpu.make_async_copy(v_hbm, kv.at[0:ROWS, HEAD : 2 * HEAD], lsem.at[1])
    load_g = pltpu.make_async_copy(g_hbm, g.at[block(x), :], lsem.at[2])
    load_q = pltpu.make_async_copy(q_hbm, q, lsem.at[3])
    load_w = [
        pltpu.make_async_copy(w_hbm.at[:, k * CW : (k + 1) * CW], w.at[:, k * CW : (k + 1) * CW], wsem.at[k])
        for k in range(NC)
    ]
    for copy in [load_k, load_v, load_g, load_q] + load_w:
        copy.start()

    barrier = pltpu.get_barrier_semaphore()
    friends = [xr, xl, zp, zq, core] + [chip_at(j) for j in range(1, 8)]
    for dev in friends:
        pl.semaphore_signal(barrier, inc=1, device_id=dev, device_id_type=MESH)
    load_k.wait()
    load_v.wait()
    load_g.wait()
    pl.semaphore_wait(barrier, len(friends))

    def slot(d):
        return pl.ds(pl.multiple_of(d * ROWS, ROWS), ROWS)

    def forward(i):
        return pltpu.make_async_remote_copy(
            src_ref=kv.at[slot(2 * (i + c)), :],
            dst_ref=kv.at[slot(2 * i + 1), :],
            send_sem=kf_s.at[i],
            recv_sem=kv_r.at[2 * i + 1],
            device_id=core,
            device_id_type=MESH,
        )

    for hop in range(1, 5):
        keep(kv.at[0:ROWS, :], kv.at[slot(2 * hop), :], kv_s.at[hop - 1], kv_r.at[2 * hop], chip_at(hop))

    @pl.when(c == 0)
    def _():
        forward(0).start()

    def acols(a):
        return pl.ds(a * AW, AW)

    def to_z(pos, a, n):
        keep(
            g.at[block(pos), acols(a)],
            g.at[pl.ds(pl.multiple_of(64 + pos * PART, PART), PART), acols(a)],
            agz_s.at[n, a],
            agz_r.at[pos, a],
            at(s + (pos // 2) * (2 - 4 * zh), tz),
        )

    for a in range(NA):
        keep(g.at[block(x), acols(a)], g.at[block(x), acols(a)], agx_s.at[0, a], agx_r.at[0, a], xr)
        keep(g.at[block(x), acols(a)], g.at[block(x), acols(a)], agx_s.at[1, a], agx_r.at[1, a], xl)
        to_z(x, a, 0)

    def ag_near(a):
        arrived(g.at[block(left), acols(a)], agx_r.at[0, a], xr, agx_s.at[0, a])
        if a % 2 == 0:
            keep(g.at[block(left), acols(a)], g.at[block(left), acols(a)], agx_s.at[2, a], agx_r.at[2, a], xr)
        to_z(left, a, 1)
        arrived(g.at[block(right), acols(a)], agx_r.at[1, a], xl, agx_s.at[1, a])
        if a % 2 == 1:
            keep(g.at[block(right), acols(a)], g.at[block(right), acols(a)], agx_s.at[2, a], agx_r.at[2, a], xl)
        to_z(right, a, 2)

    def ag_far(a):
        arrived(g.at[block(opp), acols(a)], agx_r.at[2, a], xr, agx_s.at[2, a])
        to_z(opp, a, 3)

    load_q.wait()
    for h in range(GROUP):
        part = q[:, h * HEAD : (h + 1) * HEAD]
        q4[h * HEAD : (h + 1) * HEAD, :] = part
        qt[:, h * HEAD : (h + 1) * HEAD] = part.T

    own_pos = lax.broadcasted_iota(jnp.int32, (1, ROWS), 1) + s * ROWS
    start = jnp.zeros((1, ROWS), jnp.int32)
    end = jnp.int32(0)
    for j in range(DOCS):
        end = end + docs_ref[j]
        start = jnp.where(end <= own_pos, jnp.maximum(start, end), start)
    start = jnp.concatenate([start] * GROUP, axis=1)
    key_row = lax.broadcasted_iota(jnp.int32, (ROWS, COLS), 0)
    query_row = lax.broadcasted_iota(jnp.int32, (ROWS, COLS), 1) % ROWS

    def scores(d):
        st = dot(kv[d * ROWS : (d + 1) * ROWS, 0:HEAD], qt[...]) * SCALE
        seen = key_row >= start - (s - d) * ROWS
        if d == 0:
            seen = seen & (key_row <= query_row)
        st = jnp.where(seen, st, -1e30)
        sc[d * ROWS : (d + 1) * ROWS, :] = st
        top = fold(st, jnp.max)
        mx[...] = top if d == 0 else jnp.maximum(mx[...], top)

    scores(0)
    for a in range(NA):
        ag_near(a)
        hop = a + 1
        arrived(kv.at[slot(2 * hop), :], kv_r.at[2 * hop], core, kv_s.at[hop - 1])
        if hop < 4:
            forward(hop - c).start()
        else:

            @pl.when(c == 1)
            def _():
                forward(3).start()

        scores(2 * hop)
    for i in range(4):
        ag_far(i)
        arrived(kv.at[slot(2 * i + 1), :], kv_r.at[2 * i + 1], core, kf_s.at[i])
        scores(2 * i + 1)

    peak = jnp.max(mx[...], axis=0, keepdims=True)

    def weigh(d, total):
        p = jnp.exp(sc[slot(d), :] - peak)
        pr[slot(d), :] = p.astype(BF16)
        return total + fold(p, jnp.sum)

    total = lax.fori_loop(0, SLOTS, weigh, jnp.zeros((8, COLS), F32))
    inv = 1.0 / jnp.sum(total, axis=0, keepdims=True)
    ot[...] = dot(kv[:, HEAD : 2 * HEAD], pr[...], ((0,), (0,))) * inv
    for h in range(GROUP):
        o[:, h * HEAD : (h + 1) * HEAD] = ot[:, h * HEAD : (h + 1) * HEAD].T.astype(BF16)

    def orow(base, n):
        return pl.ds(pl.multiple_of(base, 32), n)

    keep(o.at[orow(64 * (1 - zl) + 32, 32), :], oz.at[32:64, :], zh_s.at[0], zh_r.at[0], zhp)
    oz[0:32, :] = o[orow(64 * (1 - zl), 32), :]

    def ccols(k):
        return pl.ds(k * CW, CW)

    for k in range(NC):
        load_w[k].wait()

    def wcols(k):
        return pl.ds(pl.multiple_of(k * CW, CW), CW)

    mine = o[orow(64 * zl, 64), :]

    @pl.loop(0, NC)
    def _(k):
        tb[:, wcols(k)] = dot(mine, w[:, wcols(k)]).astype(BF16)

    arrived(oz.at[32:64, :], zh_r.at[0], zhp, zh_s.at[0])
    for k in range(NC):
        zs[:, ccols(k)] = dot(oz[...], w[:, ccols(k)]).astype(BF16)
        keep(zs.at[0:32, ccols(k)], rz.at[0:32, ccols(k)], a_s.at[0, k], a_r.at[0, k], zp)
        keep(zs.at[32:64, ccols(k)], rz.at[32:64, ccols(k)], a_s.at[1, k], a_r.at[1, k], zq)

    for a in range(NA):
        for pos in range(4):
            arrived(
                g.at[64 + pos * PART : 64 + (pos + 1) * PART, acols(a)], agz_r.at[pos, a], zp, agz_s.at[0, a]
            )
        part = dot(g[:, acols(a)], w[:, acols(a)], ((1,), (1,)))
        acc[...] = part if a == 0 else acc[...] + part
    dz[...] = acc[96:128, :].astype(BF16)
    far = orow(64 * (1 - zl) + 32, 32)
    keep(dz, do.at[far, :], zh_s.at[1], zh_r.at[1], zhp)
    do[orow(64 * zl, 64), :] = acc[0:64, :].astype(BF16)
    do[orow(64 * (1 - zl), 32), :] = acc[64:96, :].astype(BF16)

    def near(k):
        arrived(rz.at[0:32, ccols(k)], a_r.at[0, k], zp, a_s.at[0, k])
        arrived(rz.at[32:64, ccols(k)], a_r.at[1, k], zq, a_s.at[1, k])
        tb[:, ccols(k)] = (tb[:, ccols(k)].astype(F32) + rz[:, ccols(k)].astype(F32)).astype(BF16)
        if k % 2 == 0:
            keep(tb.at[block(opp), ccols(k)], rl.at[:, ccols(k)], rl_s.at[k], rl_r.at[k], xr)
            keep(tb.at[block(left), ccols(k)], xin.at[1, :, ccols(k)], x_s.at[1, k], x_r.at[1, k], xl)
        else:
            keep(tb.at[block(opp), ccols(k)], rl.at[:, ccols(k)], rl_s.at[k], rl_r.at[k], xl)
            keep(tb.at[block(right), ccols(k)], xin.at[0, :, ccols(k)], x_s.at[0, k], x_r.at[0, k], xr)

    def relay(k):
        arrived(rl.at[:, ccols(k)], rl_r.at[k], xr, rl_s.at[k])
        to = right if k % 2 == 0 else left
        tb[block(to), ccols(k)] = (
            tb[block(to), ccols(k)].astype(F32) + rl[:, ccols(k)].astype(F32)
        ).astype(BF16)
        if k % 2 == 0:
            keep(tb.at[block(to), ccols(k)], xin.at[0, :, ccols(k)], x_s.at[0, k], x_r.at[0, k], xr)
        else:
            keep(tb.at[block(to), ccols(k)], xin.at[1, :, ccols(k)], x_s.at[1, k], x_r.at[1, k], xl)

    def finish(k):
        arrived(xin.at[0, :, ccols(k)], x_r.at[0, k], xr, x_s.at[0, k])
        arrived(xin.at[1, :, ccols(k)], x_r.at[1, k], xl, x_s.at[1, k])
        proj_ref[:, ccols(k)] = (
            tb[block(x), ccols(k)].astype(F32)
            + xin[0, :, ccols(k)].astype(F32)
            + xin[1, :, ccols(k)].astype(F32)
        ).astype(BF16)

    def prepare():
        arrived(do.at[far, :], zh_r.at[1], zhp, zh_s.at[1])
        for h in range(GROUP):
            cols = slice(h * HEAD, (h + 1) * HEAD)
            part = (do[:, cols].astype(F32).T * inv[:, cols]).astype(BF16)
            dost[:, cols] = part
            dos4[cols, :] = part.T
        return jnp.sum(dost[...].astype(F32) * ot[...], axis=0, keepdims=True)

    def back(d, delta):
        rows = slice(d * ROWS, (d + 1) * ROWS)
        slope = dot(kv[rows, HEAD : 2 * HEAD], dost[...])
        p = pr[rows, :]
        ds = (p.astype(F32) * (slope - delta)).astype(BF16)
        dsb[rows, :] = ds
        return dot(ds, q4[...]) * SCALE, dot(p, dos4[...])

    def back_odd(d, delta):
        i = d // 2
        dk, dv = back(d, delta)
        rows = slice(d * ROWS, (d + 1) * ROWS)
        dkv[rows, 0:HEAD] = dk.astype(BF16)
        dkv[rows, HEAD : 2 * HEAD] = dv.astype(BF16)
        keep(dkv.at[rows, :], ci.at[i], ci_s.at[i], ci_r.at[i], core)

    def add_core(i, d):
        arrived(ci.at[i], ci_r.at[i], core, ci_s.at[i])
        rows = slice(d * ROWS, (d + 1) * ROWS)
        dkv[rows, :] = (dkv[rows, :].astype(F32) + ci[i].astype(F32)).astype(BF16)

    def back_even(d, delta):
        hop = d // 2
        dk, dv = back(d, delta)
        rows = slice(d * ROWS, (d + 1) * ROWS)
        dkv[rows, 0:HEAD] = dk.astype(BF16)
        dkv[rows, HEAD : 2 * HEAD] = dv.astype(BF16)
        if hop == 4:
            pl.when(c == 1)(lambda: add_core(3, d))
        elif hop == 0:
            pl.when(c == 0)(lambda: add_core(0, d))
        else:
            add_core(hop - c, d)
        if hop > 0:
            keep(dkv.at[rows, :], ri.at[hop - 1], ri_s.at[hop - 1], ri_r.at[hop - 1], chip_at(8 - hop))

    near(0)
    near(1)
    delta = prepare()
    for d in (7, 5, 3, 1):
        back_odd(d, delta)
    relay(0)
    relay(1)
    back_even(8, delta)
    back_even(6, delta)
    near(2)
    relay(2)
    back_even(4, delta)
    back_even(2, delta)
    near(3)
    relay(3)
    back_even(0, delta)
    dqt = dot(kv[:, 0:HEAD], dsb[...], ((0,), (0,))) * SCALE
    for h in range(GROUP):
        cols = slice(h * HEAD, (h + 1) * HEAD)
        dq_ref[:, cols] = dqt[:, cols].T.astype(BF16)
    for k in range(4, NC):
        near(k)
        relay(k)
        finish(k - 4)
    for k in range(NC - 4, NC):
        finish(k)

    grad = dkv[0:ROWS, :].astype(F32)
    for i in range(4):
        arrived(ri.at[i], ri_r.at[i], core, ri_s.at[i])
        grad = grad + ri[i].astype(F32)
    dk_ref[...] = grad[:, 0:HEAD].astype(BF16)
    dv_ref[...] = grad[:, HEAD : 2 * HEAD].astype(BF16)

    for copy in sent:
        copy.wait_send()
    for i in range(4):
        forward(i).wait_send()


def body(queries, key_rows, values, out_weight, out_grad, doc_lengths):
    any_spec = pl.BlockSpec(memory_space=pl.ANY)
    vmem = pl.BlockSpec(memory_space=pltpu.VMEM)
    dma = pltpu.SemaphoreType.DMA
    scratch = [
        pltpu.VMEM((COLS, D), BF16),
        pltpu.VMEM((ROWS, D), BF16),
        pltpu.VMEM((ROWS, COLS), BF16),
        pltpu.VMEM((HEAD, COLS), BF16),
        pltpu.VMEM((COLS, HEAD), BF16),
        pltpu.VMEM((SLOTS * ROWS, 2 * HEAD), BF16),
        pltpu.VMEM((SLOTS * ROWS, COLS), F32),
        pltpu.VMEM((SLOTS * ROWS, COLS), BF16),
        pltpu.VMEM((8, COLS), F32),
        pltpu.VMEM((HEAD, COLS), F32),
        pltpu.VMEM((ROWS, COLS), BF16),
        pltpu.VMEM((64, COLS), BF16),
        pltpu.VMEM((64, D), BF16),
        pltpu.VMEM((64, D), BF16),
        pltpu.VMEM((64, D), BF16),
        pltpu.VMEM((PART, D), BF16),
        pltpu.VMEM((2, PART, D), BF16),
        pltpu.VMEM((ROWS, COLS), F32),
        pltpu.VMEM((ROWS, COLS), BF16),
        pltpu.VMEM((32, COLS), BF16),
        pltpu.VMEM((HEAD, COLS), BF16),
        pltpu.VMEM((COLS, HEAD), BF16),
        pltpu.VMEM((SLOTS * ROWS, COLS), BF16),
        pltpu.VMEM((SLOTS * ROWS, 2 * HEAD), BF16),
        pltpu.VMEM((4, ROWS, 2 * HEAD), BF16),
        pltpu.VMEM((4, ROWS, 2 * HEAD), BF16),
        dma((4,)), dma((NC,)),
        dma((3, NA)), dma((3, NA)), dma((4, NA)), dma((4, NA)),
        dma((4,)), dma((SLOTS,)), dma((4,)),
        dma((2,)), dma((2,)),
        dma((2, NC)), dma((2, NC)), dma((NC,)), dma((NC,)), dma((2, NC)), dma((2, NC)),
        dma((4,)), dma((4,)), dma((4,)), dma((4,)),
    ]
    return pl.pallas_call(
        kernel,
        out_shape=(
            jax.ShapeDtypeStruct((PART, D), BF16),
            jax.ShapeDtypeStruct((ROWS, COLS), BF16),
            jax.ShapeDtypeStruct((ROWS, HEAD), BF16),
            jax.ShapeDtypeStruct((ROWS, HEAD), BF16),
        ),
        in_specs=[pl.BlockSpec(memory_space=pltpu.SMEM)] + [any_spec] * 5,
        out_specs=(vmem,) * 4,
        scratch_shapes=scratch,
        compiler_params=pltpu.CompilerParams(
            collective_id=0, has_side_effects=True, vmem_limit_bytes=48 * 1024 * 1024
        ),
    )(doc_lengths, queries, key_rows, values, out_weight, out_grad)


def solution(mesh):
    return jax.shard_map(
        body,
        mesh=mesh,
        in_specs=(
            P("seq", "tensor"),
            P("seq", "tensor"),
            P("seq", "tensor"),
            P("tensor", None),
            P(("seq", "tensor"), None),
            P(),
        ),
        out_specs=(
            P(("seq", "tensor"), None),
            P("seq", "tensor"),
            P("seq", "tensor"),
            P("seq", "tensor"),
        ),
        check_vma=False,
    )
```

time: 208 us -> 75.9 us (0.36)
  the two profiles are of different devices: /device:TPU:0 before, /device:TPU:4 now
where the time goes in v1:
time: 75.9 us; the launch traced here: 75.6 us
  Pallas kernels  68.4 us (90%)
  local copies, waits for them, and re-layouts  6.6 us (9%)
    pallas_call x1, Pallas kernels, body(): pl.pallas_call(kernel, out_shape=(jax.ShapeDtypeStruct((PART, D), BF16),...  68.4 us
    unnamed x14, local copies, waits for them, and re-layouts  6.6 us

profile of v1, /device:TPU:4, one launch (start us, length us, event | category | flops | bytes accessed | tf_op | source)
XLA Modules:
  0.0 75.6 jit_solution(11355012414846260852)
XLA Ops:
  0.6 0.0 copy-start
  0.6 0.9 %copy-done = bf16[16,8192]{1,0:T(8,128)(2,1)S(1)} copy-done((bf16[16,8192]{1,0:T(8,128)(2,1)S(1)}, bf16[16,8192]{1,0:T(8,128)(2,1)}, u32[]{:S(2)}) %copy-start) | copy-done | bytes 262168
  1.6 0.0 copy-start.1
  1.6 0.9 %copy-done.1 = bf16[128,512]{1,0:T(8,128)(2,1)S(1)} copy-done((bf16[128,512]{1,0:T(8,128)(2,1)S(1)}, bf16[128,512]{1,0:T(8,128)(2,1)}, u32[]{:S(2)}) %copy-start.1) | copy-done | bytes 131096
  2.5 0.0 copy-start.2
  2.5 0.8 copy-done.2
  3.2 0.0 copy-start.3
  3.2 0.8 copy-done.3
  4.0 0.0 copy-start.4
  4.0 0.7 copy-done.4
  4.7 68.4 %shard_map.93 = (bf16[16,8192]{1,0:T(8,128)(2,1)S(1)}, bf16[128,512]{1,0:T(8,128)(2,1)S(1)}, bf16[128,128]{1,0:T(8,128)(2,1)S(1)}, bf16[128,128]{1,0:T(8,128)(2,1)S(1)}) custom-call(s32[12]{0:T(128)S(1)} %copy-done.4, bf16[128,512]{1,0:T(8,128)(2,1)S(1)} %copy-done.1, bf16[128,128]{1,0:T(8,128)(2,1)S(1)} %copy-done.2, bf16[128,128]{1,0:T(8,128)(2,1)S(1)} %copy-done.3, ...), custom_call_target="tpu_custom_call" | custom-call | tf_op jit(solution)/shard_map/pallas_call | solution.py:410
  73.0 0.7 copy.14
  73.7 0.7 copy.15
  74.4 0.6 copy.16
  75.0 0.6 copy.17
Async XLA Ops:
  0.6 1.0 %copy-start = (bf16[16,8192]{1,0:T(8,128)(2,1)S(1)}, bf16[16,8192]{1,0:T(8,128)(2,1)}, u32[]{:S(2)}) copy-start(bf16[16,8192]{1,0:T(8,128)(2,1)} %g_hbm.1) | copy-start | bytes 786436
  1.6 0.9 %copy-start.1 = (bf16[128,512]{1,0:T(8,128)(2,1)S(1)}, bf16[128,512]{1,0:T(8,128)(2,1)}, u32[]{:S(2)}) copy-start(bf16[128,512]{1,0:T(8,128)(2,1)} %q_hbm.1) | copy-start | bytes 393220
  2.5 0.8 %copy-start.2 = (bf16[128,128]{1,0:T(8,128)(2,1)S(1)}, bf16[128,128]{1,0:T(8,128)(2,1)}, u32[]{:S(2)}) copy-start(bf16[128,128]{1,0:T(8,128)(2,1)} %k_hbm.1) | copy-start | bytes 98308
  3.2 0.8 %copy-start.3 = (bf16[128,128]{1,0:T(8,128)(2,1)S(1)}, bf16[128,128]{1,0:T(8,128)(2,1)}, u32[]{:S(2)}) copy-start(bf16[128,128]{1,0:T(8,128)(2,1)} %v_hbm.1) | copy-start | bytes 98308
  4.0 0.7 copy-start.4

commit v2 on v1

--- a/solution.py
+++ b/solution.py
@@ -15,7 +15,7 @@
 DOCS = 12
 PART = 16
 SLOTS = 9
-NA = 4
+NA = 8
 AW = D // NA
 NC = 8
 CW = D // NC
@@ -34,15 +34,15 @@
 
 
 def kernel(
-    docs_ref, q_hbm, k_hbm, v_hbm, w_hbm, g_hbm,
+    docs_hbm, q_hbm, k_hbm, v_hbm, w_hbm, g_hbm,
     proj_ref, dq_ref, dk_ref, dv_ref,
-    w, g, q, qt, q4, kv, sc, pr, mx, ot, o, oz, zs, rz, tb, rl, xin,
+    docs_ref, w, g, q, qt, q4, kv, sc, pr, mx, ot, o, oz, zs, rz, tb, xin,
     acc, do, dz, dost, dos4, dsb, dkv, ci, ri,
     lsem, wsem,
     agx_s, agx_r, agz_s, agz_r,
     kv_s, kv_r, kf_s,
     zh_s, zh_r,
-    a_s, a_r, rl_s, rl_r, x_s, x_r,
+    a_s, a_r, x_s, x_r,
     ci_s, ci_r, ri_s, ri_r,
 ):
     s, t = lax.axis_index("seq"), lax.axis_index("tensor")
@@ -55,7 +55,7 @@
     def at(seq, tensor):
         return {"seq": seq, "tensor": tensor}
 
-    xr, xl = at(s, zl * 4 + (x + 1) % 4), at(s, zl * 4 + (x + 3) % 4)
+    beside = [at(s, zl * 4 + (x + j) % 4) for j in range(4)]
     zp, zq, zhp = at(s, tz), at(sz, tz), at(sz, t)
     core = at(s + 1 - 2 * c, t)
 
@@ -84,21 +84,23 @@
 
     left, right, opp = (x + 3) % 4, (x + 1) % 4, (x + 2) % 4
 
+    barrier = pltpu.get_barrier_semaphore()
+    friends = beside[1:] + [zp, zq, core] + [chip_at(j) for j in range(1, 8)]
+    for dev in friends:
+        pl.semaphore_signal(barrier, inc=1, device_id=dev, device_id_type=MESH)
+
     load_k = pltpu.make_async_copy(k_hbm, kv.at[0:ROWS, 0:HEAD], lsem.at[0])
     load_v = pltpu.make_async_copy(v_hbm, kv.at[0:ROWS, HEAD : 2 * HEAD], lsem.at[1])
     load_g = pltpu.make_async_copy(g_hbm, g.at[block(x), :], lsem.at[2])
     load_q = pltpu.make_async_copy(q_hbm, q, lsem.at[3])
+    load_docs = pltpu.make_async_copy(docs_hbm, docs_ref, lsem.at[4])
     load_w = [
         pltpu.make_async_copy(w_hbm.at[:, k * CW : (k + 1) * CW], w.at[:, k * CW : (k + 1) * CW], wsem.at[k])
         for k in range(NC)
     ]
-    for copy in [load_k, load_v, load_g, load_q] + load_w:
+    for copy in [load_k, load_v, load_g, load_q, load_docs] + load_w:
         copy.start()
 
-    barrier = pltpu.get_barrier_semaphore()
-    friends = [xr, xl, zp, zq, core] + [chip_at(j) for j in range(1, 8)]
-    for dev in friends:
-        pl.semaphore_signal(barrier, inc=1, device_id=dev, device_id_type=MESH)
     load_k.wait()
     load_v.wait()
     load_g.wait()
@@ -137,25 +139,18 @@
         )
 
     for a in range(NA):
-        keep(g.at[block(x), acols(a)], g.at[block(x), acols(a)], agx_s.at[0, a], agx_r.at[0, a], xr)
-        keep(g.at[block(x), acols(a)], g.at[block(x), acols(a)], agx_s.at[1, a], agx_r.at[1, a], xl)
+        for j in range(1, 4):
+            keep(g.at[block(x), acols(a)], g.at[block(x), acols(a)], agx_s.at[j - 1, a], agx_r.at[j - 1, a], beside[j])
         to_z(x, a, 0)
 
-    def ag_near(a):
-        arrived(g.at[block(left), acols(a)], agx_r.at[0, a], xr, agx_s.at[0, a])
-        if a % 2 == 0:
-            keep(g.at[block(left), acols(a)], g.at[block(left), acols(a)], agx_s.at[2, a], agx_r.at[2, a], xr)
-        to_z(left, a, 1)
-        arrived(g.at[block(right), acols(a)], agx_r.at[1, a], xl, agx_s.at[1, a])
-        if a % 2 == 1:
-            keep(g.at[block(right), acols(a)], g.at[block(right), acols(a)], agx_s.at[2, a], agx_r.at[2, a], xl)
-        to_z(right, a, 2)
-
-    def ag_far(a):
-        arrived(g.at[block(opp), acols(a)], agx_r.at[2, a], xr, agx_s.at[2, a])
-        to_z(opp, a, 3)
+    def ag_step(a):
+        for j in (1, 3, 2):
+            pos = (x + 4 - j) % 4
+            arrived(g.at[block(pos), acols(a)], agx_r.at[j - 1, a], core, agx_s.at[j - 1, a])
+            to_z(pos, a, j)
 
     load_q.wait()
+    load_docs.wait()
     for h in range(GROUP):
         part = q[:, h * HEAD : (h + 1) * HEAD]
         q4[h * HEAD : (h + 1) * HEAD, :] = part
@@ -181,10 +176,7 @@
         top = fold(st, jnp.max)
         mx[...] = top if d == 0 else jnp.maximum(mx[...], top)
 
-    scores(0)
-    for a in range(NA):
-        ag_near(a)
-        hop = a + 1
+    def key_step(hop):
         arrived(kv.at[slot(2 * hop), :], kv_r.at[2 * hop], core, kv_s.at[hop - 1])
         if hop < 4:
             forward(hop - c).start()
@@ -195,10 +187,17 @@
                 forward(3).start()
 
         scores(2 * hop)
-    for i in range(4):
-        ag_far(i)
+
+    def odd_step(i):
         arrived(kv.at[slot(2 * i + 1), :], kv_r.at[2 * i + 1], core, kf_s.at[i])
         scores(2 * i + 1)
+
+    scores(0)
+    for hop in range(1, 5):
+        key_step(hop)
+        ag_step(hop - 1)
+    for i in range(4):
+        odd_step(i)
 
     peak = jnp.max(mx[...], axis=0, keepdims=True)
 
@@ -217,7 +216,6 @@
         return pl.ds(pl.multiple_of(base, 32), n)
 
     keep(o.at[orow(64 * (1 - zl) + 32, 32), :], oz.at[32:64, :], zh_s.at[0], zh_r.at[0], zhp)
-    oz[0:32, :] = o[orow(64 * (1 - zl), 32), :]
 
     def ccols(k):
         return pl.ds(k * CW, CW)
@@ -225,20 +223,30 @@
     for k in range(NC):
         load_w[k].wait()
 
-    def wcols(k):
-        return pl.ds(pl.multiple_of(k * CW, CW), CW)
+    def give(part, k):
+        rows = slice(32 * part, 32 * part + 32)
+        zs[rows, ccols(k)] = dot(oz[rows, :], w[:, ccols(k)]).astype(BF16)
+        keep(
+            zs.at[rows, ccols(k)], rz.at[rows, ccols(k)], a_s.at[part, k], a_r.at[part, k], zq if part else zp
+        )
 
     mine = o[orow(64 * zl, 64), :]
 
-    @pl.loop(0, NC)
-    def _(k):
-        tb[:, wcols(k)] = dot(mine, w[:, wcols(k)]).astype(BF16)
-
+    def own(k):
+        tb[:, ccols(k)] = dot(mine, w[:, ccols(k)]).astype(BF16)
+
+    oz[0:32, :] = o[orow(64 * (1 - zl), 32), :]
+    ag_step(4)
+    ag_step(5)
+    for k in range(NC):
+        give(0, k)
+    ag_step(6)
+    for k in range(NC):
+        own(k)
+    ag_step(7)
     arrived(oz.at[32:64, :], zh_r.at[0], zhp, zh_s.at[0])
     for k in range(NC):
-        zs[:, ccols(k)] = dot(oz[...], w[:, ccols(k)]).astype(BF16)
-        keep(zs.at[0:32, ccols(k)], rz.at[0:32, ccols(k)], a_s.at[0, k], a_r.at[0, k], zp)
-        keep(zs.at[32:64, ccols(k)], rz.at[32:64, ccols(k)], a_s.at[1, k], a_r.at[1, k], zq)
+        give(1, k)
 
     for a in range(NA):
         for pos in range(4):
@@ -253,36 +261,33 @@
     do[orow(64 * zl, 64), :] = acc[0:64, :].astype(BF16)
     do[orow(64 * (1 - zl), 32), :] = acc[64:96, :].astype(BF16)
 
-    def near(k):
-        arrived(rz.at[0:32, ccols(k)], a_r.at[0, k], zp, a_s.at[0, k])
-        arrived(rz.at[32:64, ccols(k)], a_r.at[1, k], zq, a_s.at[1, k])
-        tb[:, ccols(k)] = (tb[:, ccols(k)].astype(F32) + rz[:, ccols(k)].astype(F32)).astype(BF16)
-        if k % 2 == 0:
-            keep(tb.at[block(opp), ccols(k)], rl.at[:, ccols(k)], rl_s.at[k], rl_r.at[k], xr)
-            keep(tb.at[block(left), ccols(k)], xin.at[1, :, ccols(k)], x_s.at[1, k], x_r.at[1, k], xl)
-        else:
-            keep(tb.at[block(opp), ccols(k)], rl.at[:, ccols(k)], rl_s.at[k], rl_r.at[k], xl)
-            keep(tb.at[block(right), ccols(k)], xin.at[0, :, ccols(k)], x_s.at[0, k], x_r.at[0, k], xr)
-
-    def relay(k):
-        arrived(rl.at[:, ccols(k)], rl_r.at[k], xr, rl_s.at[k])
-        to = right if k % 2 == 0 else left
-        tb[block(to), ccols(k)] = (
-            tb[block(to), ccols(k)].astype(F32) + rl[:, ccols(k)].astype(F32)
-        ).astype(BF16)
-        if k % 2 == 0:
-            keep(tb.at[block(to), ccols(k)], xin.at[0, :, ccols(k)], x_s.at[0, k], x_r.at[0, k], xr)
-        else:
-            keep(tb.at[block(to), ccols(k)], xin.at[1, :, ccols(k)], x_s.at[1, k], x_r.at[1, k], xl)
+    def near(part, k):
+        rows = slice(32 * part, 32 * part + 32)
+        arrived(rz.at[rows, ccols(k)], a_r.at[part, k], zp, a_s.at[part, k])
+        tb[rows, ccols(k)] = (tb[rows, ccols(k)].astype(F32) + rz[rows, ccols(k)].astype(F32)).astype(BF16)
+        for to in (2 * part, 2 * part + 1):
+
+            @pl.when(x != to)
+            def _():
+                x_copy(to, k).start()
+
+    def x_copy(to, k):
+        return pltpu.make_async_remote_copy(
+            src_ref=tb.at[to * PART : (to + 1) * PART, ccols(k)],
+            dst_ref=xin.at[x, :, ccols(k)],
+            send_sem=x_s.at[to, k],
+            recv_sem=x_r.at[x, k],
+            device_id=at(s, zl * 4 + to),
+            device_id_type=MESH,
+        )
 
     def finish(k):
-        arrived(xin.at[0, :, ccols(k)], x_r.at[0, k], xr, x_s.at[0, k])
-        arrived(xin.at[1, :, ccols(k)], x_r.at[1, k], xl, x_s.at[1, k])
-        proj_ref[:, ccols(k)] = (
-            tb[block(x), ccols(k)].astype(F32)
-            + xin[0, :, ccols(k)].astype(F32)
-            + xin[1, :, ccols(k)].astype(F32)
-        ).astype(BF16)
+        total = tb[block(x), ccols(k)].astype(F32)
+        for j in (1, 3, 2):
+            pos = (x + j) % 4
+            arrived(xin.at[pos, :, ccols(k)], x_r.at[pos, k], core, x_s.at[pos, k])
+            total = total + xin[pos, :, ccols(k)].astype(F32)
+        proj_ref[:, ccols(k)] = total.astype(BF16)
 
     def prepare():
         arrived(do.at[far, :], zh_r.at[1], zhp, zh_s.at[1])
@@ -329,31 +334,35 @@
         if hop > 0:
             keep(dkv.at[rows, :], ri.at[hop - 1], ri_s.at[hop - 1], ri_r.at[hop - 1], chip_at(8 - hop))
 
-    near(0)
-    near(1)
+    for k in range(4):
+        near(0, k)
+        near(1, k)
     delta = prepare()
     for d in (7, 5, 3, 1):
         back_odd(d, delta)
-    relay(0)
-    relay(1)
-    back_even(8, delta)
-    back_even(6, delta)
-    near(2)
-    relay(2)
-    back_even(4, delta)
-    back_even(2, delta)
-    near(3)
-    relay(3)
+    for d in (8, 6, 4, 2):
+        back_even(d, delta)
+    for k in range(4, NC):
+        near(0, k)
+        near(1, k)
     back_even(0, delta)
     dqt = dot(kv[:, 0:HEAD], dsb[...], ((0,), (0,))) * SCALE
     for h in range(GROUP):
         cols = slice(h * HEAD, (h + 1) * HEAD)
         dq_ref[:, cols] = dqt[:, cols].T.astype(BF16)
-    for k in range(4, NC):
-        near(k)
-        relay(k)
-        finish(k - 4)
-    for k in range(NC - 4, NC):
+
+    for copy in sent:
+        copy.wait_send()
+    for i in range(4):
+        forward(i).wait_send()
+    for to in range(4):
+
+        @pl.when(x != to)
+        def _():
+            for k in range(NC):
+                x_copy(to, k).wait_send()
+
+    for k in range(NC):
         finish(k)
 
     grad = dkv[0:ROWS, :].astype(F32)
@@ -363,17 +372,21 @@
     dk_ref[...] = grad[:, 0:HEAD].astype(BF16)
     dv_ref[...] = grad[:, HEAD : 2 * HEAD].astype(BF16)
 
-    for copy in sent:
-        copy.wait_send()
-    for i in range(4):
-        forward(i).wait_send()
+
+def store(*refs):
+    copies = [pltpu.make_async_copy(refs[i], refs[4 + i], refs[8].at[i]) for i in range(4)]
+    for copy in copies:
+        copy.start()
+    for copy in copies:
+        copy.wait()
 
 
 def body(queries, key_rows, values, out_weight, out_grad, doc_lengths):
-    any_spec = pl.BlockSpec(memory_space=pl.ANY)
+    hbm = pl.BlockSpec(memory_space=pltpu.HBM)
     vmem = pl.BlockSpec(memory_space=pltpu.VMEM)
     dma = pltpu.SemaphoreType.DMA
     scratch = [
+        pltpu.SMEM((DOCS,), jnp.int32),
         pltpu.VMEM((COLS, D), BF16),
         pltpu.VMEM((ROWS, D), BF16),
         pltpu.VMEM((ROWS, COLS), BF16),
@@ -389,8 +402,7 @@
         pltpu.VMEM((64, D), BF16),
         pltpu.VMEM((64, D), BF16),
         pltpu.VMEM((64, D), BF16),
-        pltpu.VMEM((PART, D), BF16),
-        pltpu.VMEM((2, PART, D), BF16),
+        pltpu.VMEM((4, PART, D), BF16),
         pltpu.VMEM((ROWS, COLS), F32),
         pltpu.VMEM((ROWS, COLS), BF16),
         pltpu.VMEM((32, COLS), BF16),
@@ -400,28 +412,36 @@
         pltpu.VMEM((SLOTS * ROWS, 2 * HEAD), BF16),
         pltpu.VMEM((4, ROWS, 2 * HEAD), BF16),
         pltpu.VMEM((4, ROWS, 2 * HEAD), BF16),
-        dma((4,)), dma((NC,)),
+        dma((5,)), dma((NC,)),
         dma((3, NA)), dma((3, NA)), dma((4, NA)), dma((4, NA)),
         dma((4,)), dma((SLOTS,)), dma((4,)),
         dma((2,)), dma((2,)),
-        dma((2, NC)), dma((2, NC)), dma((NC,)), dma((NC,)), dma((2, NC)), dma((2, NC)),
+        dma((2, NC)), dma((2, NC)), dma((4, NC)), dma((4, NC)),
         dma((4,)), dma((4,)), dma((4,)), dma((4,)),
     ]
-    return pl.pallas_call(
+    shapes = (
+        jax.ShapeDtypeStruct((PART, D), BF16),
+        jax.ShapeDtypeStruct((ROWS, COLS), BF16),
+        jax.ShapeDtypeStruct((ROWS, HEAD), BF16),
+        jax.ShapeDtypeStruct((ROWS, HEAD), BF16),
+    )
+    results = pl.pallas_call(
         kernel,
-        out_shape=(
-            jax.ShapeDtypeStruct((PART, D), BF16),
-            jax.ShapeDtypeStruct((ROWS, COLS), BF16),
-            jax.ShapeDtypeStruct((ROWS, HEAD), BF16),
-            jax.ShapeDtypeStruct((ROWS, HEAD), BF16),
-        ),
-        in_specs=[pl.BlockSpec(memory_space=pltpu.SMEM)] + [any_spec] * 5,
+        out_shape=shapes,
+        in_specs=[hbm] * 6,
         out_specs=(vmem,) * 4,
         scratch_shapes=scratch,
         compiler_params=pltpu.CompilerParams(
-            collective_id=0, has_side_effects=True, vmem_limit_bytes=48 * 1024 * 1024
+            collective_id=0, has_side_effects=True, vmem_limit_bytes=63 * 1024 * 1024
         ),
     )(doc_lengths, queries, key_rows, values, out_weight, out_grad)
+    return pl.pallas_call(
+        store,
+        out_shape=shapes,
+        in_specs=[vmem] * 4,
+        out_specs=(hbm,) * 4,
+        scratch_shapes=[dma((4,))],
+    )(*results)
 
 
 def solution(mesh):

time: 75.9 us -> 59.4 us (0.78)
  the two profiles are of different devices: /device:TPU:4 before, /device:TPU:1 now
where the time goes in v2:
time: 59.4 us; the launch traced here: 59.3 us
  Pallas kernels  58.6 us (99%)
  between operations  0.64 us (1%)
    pallas_call x1, Pallas kernels, body(): pl.pallas_call(kernel, out_shape=shapes, in_specs=[hbm] * 6, out_specs=(v...  56.8 us
    pallas_call x1, Pallas kernels, body(): pl.pallas_call(store, out_shape=shapes, in_specs=[vmem] * 4, out_specs=(h...  1.82 us

profile of v2, /device:TPU:1, one launch (start us, length us, event | category | flops | bytes accessed | tf_op | source)
XLA Modules:
  0.0 59.3 jit_solution(14841585799089020742)
XLA Ops:
  0.6 56.8 %shard_map.93 = (bf16[16,8192]{1,0:T(8,128)(2,1)}, bf16[128,512]{1,0:T(8,128)(2,1)}, bf16[128,128]{1,0:T(8,128)(2,1)}, bf16[128,128]{1,0:T(8,128)(2,1)}) custom-call(s32[12]{0:T(128)} %docs_hbm.1, bf16[128,512]{1,0:T(8,128)(2,1)} %q_hbm.1, bf16[128,128]{1,0:T(8,128)(2,1)} %k_hbm.1, bf16[128,128]{1,0:T(8,128)(2,1)} %v_hbm.1, bf16[512,8192]{1,0:T(8,128)(2,1)} %w_hbm.1, ...), custom_call_target="tpu_custom_call" | custom-call | tf_op jit(solution)/shard_map/pallas_call | solution.py:428
  57.5 1.8 %shard_map.94 = (bf16[16,8192]{1,0:T(8,128)(2,1)}, bf16[128,512]{1,0:T(8,128)(2,1)}, bf16[128,128]{1,0:T(8,128)(2,1)}, bf16[128,128]{1,0:T(8,128)(2,1)}) custom-call(bf16[16,8192]{1,0:T(8,128)(2,1)} %get-tuple-element.8.refs_0_, bf16[128,512]{1,0:T(8,128)(2,1)} %get-tuple-element.9.refs_1_, bf16[128,128]{1,0:T(8,128)(2,1)} %get-tuple-element.10.refs_2_, ...), custom_call_target="tpu_custom_call" | custom-call | tf_op jit(solution)/shard_map/pallas_call | solution.py:438

commit v3 on v2

--- a/solution.py
+++ b/solution.py
@@ -15,9 +15,10 @@
 DOCS = 12
 PART = 16
 SLOTS = 9
-NA = 8
+NA = 4
 AW = D // NA
-NC = 8
+NC = 4
+XFIRST = (0,)
 CW = D // NC
 SCALE = 1.0 / math.sqrt(HEAD)
 MESH = pl.DeviceIdType.MESH
@@ -36,14 +37,14 @@
 def kernel(
     docs_hbm, q_hbm, k_hbm, v_hbm, w_hbm, g_hbm,
     proj_ref, dq_ref, dk_ref, dv_ref,
-    docs_ref, w, g, q, qt, q4, kv, sc, pr, mx, ot, o, oz, zs, rz, tb, xin,
-    acc, do, dz, dost, dos4, dsb, dkv, ci, ri,
+    docs_ref, w, g, q, qt, q4, kv, sc, pr, mx, ot, o, oz, zs, rz, tb, xin, yin, ym, zin,
+    acc, do, dz, dost, dos4, dsb, dkv, ci, fi, ri, rj, st,
     lsem, wsem,
     agx_s, agx_r, agz_s, agz_r,
     kv_s, kv_r, kf_s,
     zh_s, zh_r,
-    a_s, a_r, x_s, x_r,
-    ci_s, ci_r, ri_s, ri_r,
+    a_s, a_r, x_s, x_r, y_s, y_r, m_s, m_r,
+    ci_s, ci_r, fi_s, fi_r, ri_s, ri_r, rj_s, rj_r,
 ):
     s, t = lax.axis_index("seq"), lax.axis_index("tensor")
     c, chip = s % 2, s // 2
@@ -85,7 +86,7 @@
     left, right, opp = (x + 3) % 4, (x + 1) % 4, (x + 2) % 4
 
     barrier = pltpu.get_barrier_semaphore()
-    friends = beside[1:] + [zp, zq, core] + [chip_at(j) for j in range(1, 8)]
+    friends = beside[1:] + [zp, zq, zhp, core] + [chip_at(j) for j in (2, 4, 6)]
     for dev in friends:
         pl.semaphore_signal(barrier, inc=1, device_id=dev, device_id_type=MESH)
 
@@ -119,12 +120,38 @@
             device_id_type=MESH,
         )
 
-    for hop in range(1, 5):
-        keep(kv.at[0:ROWS, :], kv.at[slot(2 * hop), :], kv_s.at[hop - 1], kv_r.at[2 * hop], chip_at(hop))
+    def flip():
+        return pltpu.make_async_remote_copy(
+            src_ref=kv.at[0:ROWS, :],
+            dst_ref=kv.at[slot(2 + 7 * zh), :],
+            send_sem=kv_s.at[2],
+            recv_sem=kv_r.at[2 + 7 * zh],
+            device_id=zhp,
+            device_id_type=MESH,
+        )
+
+    def pass_on(i):
+        return pltpu.make_async_remote_copy(
+            src_ref=kv.at[slot(9 - 7 * zh), :],
+            dst_ref=kv.at[slot(6 if i else 2 + 4 * zh), :],
+            send_sem=kv_s.at[3 + i],
+            recv_sem=kv_r.at[6 if i else 2 + 4 * zh],
+            device_id=chip_at(4 if i else 2),
+            device_id_type=MESH,
+        )
+
+    flip().start()
+    for i in range(2):
+        keep(kv.at[0:ROWS, :], kv.at[slot(4 * i + 4), :], kv_s.at[i], kv_r.at[4 * i + 4], chip_at(2 * i + 2))
 
     @pl.when(c == 0)
     def _():
         forward(0).start()
+
+    def orow(base, n):
+        return pl.ds(pl.multiple_of(base, 32), n)
+
+    far = orow(64 * (1 - zl) + 32, 32)
 
     def acols(a):
         return pl.ds(a * AW, AW)
@@ -141,13 +168,15 @@
     for a in range(NA):
         for j in range(1, 4):
             keep(g.at[block(x), acols(a)], g.at[block(x), acols(a)], agx_s.at[j - 1, a], agx_r.at[j - 1, a], beside[j])
-        to_z(x, a, 0)
+
+    def ag_part(a, j):
+        pos = (x + 4 - j) % 4
+        arrived(g.at[block(pos), acols(a)], agx_r.at[j - 1, a], core, agx_s.at[j - 1, a])
+        to_z(pos, a, j)
 
     def ag_step(a):
         for j in (1, 3, 2):
-            pos = (x + 4 - j) % 4
-            arrived(g.at[block(pos), acols(a)], agx_r.at[j - 1, a], core, agx_s.at[j - 1, a])
-            to_z(pos, a, j)
+            ag_part(a, j)
 
     load_q.wait()
     load_docs.wait()
@@ -176,8 +205,22 @@
         top = fold(st, jnp.max)
         mx[...] = top if d == 0 else jnp.maximum(mx[...], top)
 
+    def flip_step():
+        arrived(kv.at[slot(9 - 7 * zh), :], kv_r.at[9 - 7 * zh], core, kv_s.at[0])
+        pass_on(0).start()
+
+        @pl.when(zh == 0)
+        def _():
+            pass_on(1).start()
+
     def key_step(hop):
-        arrived(kv.at[slot(2 * hop), :], kv_r.at[2 * hop], core, kv_s.at[hop - 1])
+        if hop == 1:
+
+            @pl.when(zh == 0)
+            def _():
+                arrived(kv.at[slot(2), :], kv_r.at[2], core, kv_s.at[0])
+        else:
+            arrived(kv.at[slot(2 * hop), :], kv_r.at[2 * hop], core, kv_s.at[0])
         if hop < 4:
             forward(hop - c).start()
         else:
@@ -192,74 +235,64 @@
         arrived(kv.at[slot(2 * i + 1), :], kv_r.at[2 * i + 1], core, kf_s.at[i])
         scores(2 * i + 1)
 
-    scores(0)
-    for hop in range(1, 5):
-        key_step(hop)
-        ag_step(hop - 1)
-    for i in range(4):
-        odd_step(i)
-
-    peak = jnp.max(mx[...], axis=0, keepdims=True)
-
-    def weigh(d, total):
-        p = jnp.exp(sc[slot(d), :] - peak)
-        pr[slot(d), :] = p.astype(BF16)
-        return total + fold(p, jnp.sum)
-
-    total = lax.fori_loop(0, SLOTS, weigh, jnp.zeros((8, COLS), F32))
-    inv = 1.0 / jnp.sum(total, axis=0, keepdims=True)
-    ot[...] = dot(kv[:, HEAD : 2 * HEAD], pr[...], ((0,), (0,))) * inv
-    for h in range(GROUP):
-        o[:, h * HEAD : (h + 1) * HEAD] = ot[:, h * HEAD : (h + 1) * HEAD].T.astype(BF16)
-
-    def orow(base, n):
-        return pl.ds(pl.multiple_of(base, 32), n)
-
-    keep(o.at[orow(64 * (1 - zl) + 32, 32), :], oz.at[32:64, :], zh_s.at[0], zh_r.at[0], zhp)
-
     def ccols(k):
         return pl.ds(k * CW, CW)
 
-    for k in range(NC):
-        load_w[k].wait()
+    given = {}
 
     def give(part, k):
         rows = slice(32 * part, 32 * part + 32)
         zs[rows, ccols(k)] = dot(oz[rows, :], w[:, ccols(k)]).astype(BF16)
-        keep(
+        given[part, k] = send(
             zs.at[rows, ccols(k)], rz.at[rows, ccols(k)], a_s.at[part, k], a_r.at[part, k], zq if part else zp
         )
-
-    mine = o[orow(64 * zl, 64), :]
 
     def own(k):
         tb[:, ccols(k)] = dot(mine, w[:, ccols(k)]).astype(BF16)
-
-    oz[0:32, :] = o[orow(64 * (1 - zl), 32), :]
-    ag_step(4)
-    ag_step(5)
-    for k in range(NC):
-        give(0, k)
-    ag_step(6)
-    for k in range(NC):
-        own(k)
-    ag_step(7)
-    arrived(oz.at[32:64, :], zh_r.at[0], zhp, zh_s.at[0])
-    for k in range(NC):
-        give(1, k)
-
-    for a in range(NA):
+        if k in XFIRST:
+            for to in range(4):
+
+                @pl.when(x != to)
+                def _():
+                    x_copy(to, k).start()
+
+    def spread(part, k):
+        rows = slice(32 * part, 32 * part + 32)
+        zs[rows, ccols(k)] = dot(oz[rows, :], w[:, ccols(k)]).astype(BF16)
+        for to in (2 * part, 2 * part + 1):
+
+            @pl.when(x != to)
+            def _():
+                y_copy(to, k).start()
+
+    def y_copy(to, k):
+        return pltpu.make_async_remote_copy(
+            src_ref=zs.at[to * PART : (to + 1) * PART, ccols(k)],
+            dst_ref=yin.at[x, :, ccols(k)],
+            send_sem=y_s.at[to, k],
+            recv_sem=y_r.at[x, k],
+            device_id=at(s, zl * 4 + to),
+            device_id_type=MESH,
+        )
+
+    def middle(k):
+        total = zs[block(x), ccols(k)].astype(F32)
+        for j in (1, 3, 2):
+            pos = (x + j) % 4
+            arrived(yin.at[pos, :, ccols(k)], y_r.at[pos, k], core, y_s.at[pos, k])
+            total = total + yin[pos, :, ccols(k)].astype(F32)
+        ym[:, ccols(k)] = total.astype(BF16)
+        keep(
+            ym.at[:, ccols(k)], zin.at[:, ccols(k)], m_s.at[k], m_r.at[k], at(s + (x // 2) * (2 - 4 * zh), tz)
+        )
+
+    def attn_grad(a):
         for pos in range(4):
             arrived(
                 g.at[64 + pos * PART : 64 + (pos + 1) * PART, acols(a)], agz_r.at[pos, a], zp, agz_s.at[0, a]
             )
         part = dot(g[:, acols(a)], w[:, acols(a)], ((1,), (1,)))
         acc[...] = part if a == 0 else acc[...] + part
-    dz[...] = acc[96:128, :].astype(BF16)
-    far = orow(64 * (1 - zl) + 32, 32)
-    keep(dz, do.at[far, :], zh_s.at[1], zh_r.at[1], zhp)
-    do[orow(64 * zl, 64), :] = acc[0:64, :].astype(BF16)
-    do[orow(64 * (1 - zl), 32), :] = acc[64:96, :].astype(BF16)
 
     def near(part, k):
         rows = slice(32 * part, 32 * part + 32)
@@ -283,6 +316,9 @@
 
     def finish(k):
         total = tb[block(x), ccols(k)].astype(F32)
+        if k in XFIRST:
+            arrived(zin.at[:, ccols(k)], m_r.at[k], core, m_s.at[k])
+            total = total + zin[:, ccols(k)].astype(F32)
         for j in (1, 3, 2):
             pos = (x + j) % 4
             arrived(xin.at[pos, :, ccols(k)], x_r.at[pos, k], core, x_s.at[pos, k])
@@ -331,47 +367,154 @@
             pl.when(c == 0)(lambda: add_core(0, d))
         else:
             add_core(hop - c, d)
-        if hop > 0:
-            keep(dkv.at[rows, :], ri.at[hop - 1], ri_s.at[hop - 1], ri_r.at[hop - 1], chip_at(8 - hop))
-
-    for k in range(4):
-        near(0, k)
-        near(1, k)
+        if hop % 2 == 0 and hop > 0:
+            i = hop // 2 - 1
+            keep(dkv.at[rows, :], ri.at[i], ri_s.at[i], ri_r.at[i], chip_at(6 - 2 * i))
+
+    def hand_back(i):
+        return pltpu.make_async_remote_copy(
+            src_ref=dkv.at[slot(6 if i else 2 + 4 * zh), :],
+            dst_ref=rj.at[i],
+            send_sem=rj_s.at[i],
+            recv_sem=rj_r.at[i],
+            device_id=chip_at(4 if i else 6),
+            device_id_type=MESH,
+        )
+
+    def flip_back():
+        arrived(rj.at[0], rj_r.at[0], core, rj_s.at[0])
+
+        @pl.when(zh == 0)
+        def _():
+            arrived(rj.at[1], rj_r.at[1], core, rj_s.at[1])
+            st[...] = (rj[0].astype(F32) + rj[1].astype(F32)).astype(BF16)
+
+        @pl.when(zh == 1)
+        def _():
+            st[...] = (rj[0].astype(F32) + dkv[2 * ROWS : 3 * ROWS, :].astype(F32)).astype(BF16)
+
+        keep(st, fi, fi_s.at[0], fi_r.at[0], zhp)
+
+    for a in range(NA):
+        to_z(x, a, 0)
+    scores(0)
+    flip_step()
+    key_step(2)
+    key_step(4)
+    ag_step(0)
+    ag_step(1)
+    key_step(1)
+    key_step(3)
+    odd_step(1)
+    odd_step(0)
+    odd_step(3)
+    odd_step(2)
+    ag_step(2)
+    peak = jnp.max(mx[...], axis=0, keepdims=True)
+
+    def weigh(d, total):
+        p = jnp.exp(sc[slot(d), :] - peak)
+        pr[slot(d), :] = p.astype(BF16)
+        return total + fold(p, jnp.sum)
+
+    total = lax.fori_loop(0, SLOTS, weigh, jnp.zeros((8, COLS), F32))
+    inv = 1.0 / jnp.sum(total, axis=0, keepdims=True)
+    ot[...] = dot(kv[0 : SLOTS * ROWS, HEAD : 2 * HEAD], pr[...], ((0,), (0,))) * inv
+    for h in range(GROUP):
+        o[:, h * HEAD : (h + 1) * HEAD] = ot[:, h * HEAD : (h + 1) * HEAD].T.astype(BF16)
+
+    keep(o.at[orow(64 * (1 - zl) + 32, 32), :], oz.at[32:64, :], zh_s.at[0], zh_r.at[0], zhp)
+
+    for k in range(NC):
+        load_w[k].wait()
+
+    mine = o[orow(64 * zl, 64), :]
+
+    oz[0:32, :] = o[orow(64 * (1 - zl), 32), :]
+    ag_step(3)
+    own(0)
+    spread(0, 0)
+    own(1)
+    own(2)
+    own(3)
+    give(0, 1)
+    arrived(oz.at[32:64, :], zh_r.at[0], zhp, zh_s.at[0])
+    spread(1, 0)
+    give(1, 1)
+    attn_grad(0)
+    attn_grad(1)
+    attn_grad(2)
+    attn_grad(3)
+    dz[...] = acc[96:128, :].astype(BF16)
+    keep(dz, do.at[far, :], zh_s.at[1], zh_r.at[1], zhp)
+    do[orow(64 * zl, 64), :] = acc[0:64, :].astype(BF16)
+    do[orow(64 * (1 - zl), 32), :] = acc[64:96, :].astype(BF16)
+    give(0, 2)
+    give(1, 2)
+    give(0, 3)
+    give(1, 3)
+    middle(0)
+    near(0, 1)
+    near(1, 1)
     delta = prepare()
-    for d in (7, 5, 3, 1):
-        back_odd(d, delta)
-    for d in (8, 6, 4, 2):
-        back_even(d, delta)
-    for k in range(4, NC):
-        near(0, k)
-        near(1, k)
+    back_odd(7, delta)
+    back_odd(5, delta)
+    back_odd(3, delta)
+    back_odd(1, delta)
+    back_even(6, delta)
+    back_even(2, delta)
+    hand_back(0).start()
+
+    @pl.when(zh == 0)
+    def _():
+        hand_back(1).start()
+
+    near(0, 2)
+    back_even(8, delta)
+    near(1, 2)
+    back_even(4, delta)
     back_even(0, delta)
-    dqt = dot(kv[:, 0:HEAD], dsb[...], ((0,), (0,))) * SCALE
+    near(0, 3)
+    flip_back()
+    near(1, 3)
+    dqt = dot(kv[0 : SLOTS * ROWS, 0:HEAD], dsb[...], ((0,), (0,))) * SCALE
     for h in range(GROUP):
         cols = slice(h * HEAD, (h + 1) * HEAD)
         dq_ref[:, cols] = dqt[:, cols].T.astype(BF16)
-
+    for copy in given.values():
+        copy.wait_send()
     for copy in sent:
         copy.wait_send()
     for i in range(4):
         forward(i).wait_send()
+    flip().wait_send()
+    pass_on(0).wait_send()
+    hand_back(0).wait_send()
+
+    @pl.when(zh == 0)
+    def _():
+        pass_on(1).wait_send()
+        hand_back(1).wait_send()
+
     for to in range(4):
 
         @pl.when(x != to)
         def _():
             for k in range(NC):
                 x_copy(to, k).wait_send()
-
+            for k in XFIRST:
+                y_copy(to, k).wait_send()
     for k in range(NC):
         finish(k)
 
     grad = dkv[0:ROWS, :].astype(F32)
-    for i in range(4):
+    arrived(fi, fi_r.at[0], zhp, fi_s.at[0])
+    grad = grad + fi[...].astype(F32)
+    for i in range(2):
         arrived(ri.at[i], ri_r.at[i], core, ri_s.at[i])
         grad = grad + ri[i].astype(F32)
     dk_ref[...] = grad[:, 0:HEAD].astype(BF16)
     dv_ref[...] = grad[:, HEAD : 2 * HEAD].astype(BF16)
-
 
 def store(*refs):
     copies = [pltpu.make_async_copy(refs[i], refs[4 + i], refs[8].at[i]) for i in range(4)]
@@ -392,7 +535,7 @@
         pltpu.VMEM((ROWS, COLS), BF16),
         pltpu.VMEM((HEAD, COLS), BF16),
         pltpu.VMEM((COLS, HEAD), BF16),
-        pltpu.VMEM((SLOTS * ROWS, 2 * HEAD), BF16),
+        pltpu.VMEM(((SLOTS + 1) * ROWS, 2 * HEAD), BF16),
         pltpu.VMEM((SLOTS * ROWS, COLS), F32),
         pltpu.VMEM((SLOTS * ROWS, COLS), BF16),
         pltpu.VMEM((8, COLS), F32),
@@ -403,6 +546,9 @@
         pltpu.VMEM((64, D), BF16),
         pltpu.VMEM((64, D), BF16),
         pltpu.VMEM((4, PART, D), BF16),
+        pltpu.VMEM((4, PART, D), BF16),
+        pltpu.VMEM((PART, D), BF16),
+        pltpu.VMEM((PART, D), BF16),
         pltpu.VMEM((ROWS, COLS), F32),
         pltpu.VMEM((ROWS, COLS), BF16),
         pltpu.VMEM((32, COLS), BF16),
@@ -411,13 +557,17 @@
         pltpu.VMEM((SLOTS * ROWS, COLS), BF16),
         pltpu.VMEM((SLOTS * ROWS, 2 * HEAD), BF16),
         pltpu.VMEM((4, ROWS, 2 * HEAD), BF16),
-        pltpu.VMEM((4, ROWS, 2 * HEAD), BF16),
+        pltpu.VMEM((ROWS, 2 * HEAD), BF16),
+        pltpu.VMEM((2, ROWS, 2 * HEAD), BF16),
+        pltpu.VMEM((2, ROWS, 2 * HEAD), BF16),
+        pltpu.VMEM((ROWS, 2 * HEAD), BF16),
         dma((5,)), dma((NC,)),
         dma((3, NA)), dma((3, NA)), dma((4, NA)), dma((4, NA)),
-        dma((4,)), dma((SLOTS,)), dma((4,)),
+        dma((5,)), dma((SLOTS + 1,)), dma((4,)),
         dma((2,)), dma((2,)),
         dma((2, NC)), dma((2, NC)), dma((4, NC)), dma((4, NC)),
-        dma((4,)), dma((4,)), dma((4,)), dma((4,)),
+        dma((4, NC)), dma((4, NC)), dma((NC,)), dma((NC,)),
+        dma((4,)), dma((4,)), dma((1,)), dma((1,)), dma((2,)), dma((2,)), dma((2,)), dma((2,)),
     ]
     shapes = (
         jax.ShapeDtypeStruct((PART, D), BF16),

time: 59.4 us -> 48.7 us (0.82)
  Pallas kernels: 58.6 us -> 47.9 us
    pallas_call x1, Pallas kernels: 56.8 us -> 46.1 us  [body(): pl.pallas_call(kernel, out_shape=shapes, in_specs=[hbm] * 6, out_specs=(v...]
where the time goes in v3:
time: 48.7 us; the launch traced here: 48.6 us
  Pallas kernels  47.9 us (98%)
  between operations  0.64 us (1%)
    pallas_call x1, Pallas kernels, body(): pl.pallas_call(kernel, out_shape=shapes, in_specs=[hbm] * 6, out_specs=(v...  46.1 us
    pallas_call x1, Pallas kernels, body(): pl.pallas_call(store, out_shape=shapes, in_specs=[vmem] * 4, out_specs=(h...  1.82 us

profile of v3, /device:TPU:1, one launch (start us, length us, event | category | flops | bytes accessed | tf_op | source)
XLA Modules:
  0.0 48.6 jit_solution(6621738555284531521)
XLA Ops:
  0.6 46.1 %shard_map.93 = (bf16[16,8192]{1,0:T(8,128)(2,1)}, bf16[128,512]{1,0:T(8,128)(2,1)}, bf16[128,128]{1,0:T(8,128)(2,1)}, bf16[128,128]{1,0:T(8,128)(2,1)}) custom-call(s32[12]{0:T(128)} %docs_hbm.1, bf16[128,512]{1,0:T(8,128)(2,1)} %q_hbm.1, bf16[128,128]{1,0:T(8,128)(2,1)} %k_hbm.1, bf16[128,128]{1,0:T(8,128)(2,1)} %v_hbm.1, bf16[512,8192]{1,0:T(8,128)(2,1)} %w_hbm.1, ...), custom_call_target="tpu_custom_call" | custom-call | tf_op jit(solution)/shard_map/pallas_call | solution.py:578
  46.7 1.8 %shard_map.94 = (bf16[16,8192]{1,0:T(8,128)(2,1)}, bf16[128,512]{1,0:T(8,128)(2,1)}, bf16[128,128]{1,0:T(8,128)(2,1)}, bf16[128,128]{1,0:T(8,128)(2,1)}) custom-call(bf16[16,8192]{1,0:T(8,128)(2,1)} %get-tuple-element.8.refs_0_, bf16[128,512]{1,0:T(8,128)(2,1)} %get-tuple-element.9.refs_1_, bf16[128,128]{1,0:T(8,128)(2,1)} %get-tuple-element.10.refs_2_, ...), custom_call_target="tpu_custom_call" | custom-call | tf_op jit(solution)/shard_map/pallas_call | solution.py:588

commit v4 on v3

--- a/solution.py
+++ b/solution.py
@@ -40,7 +40,7 @@
     docs_ref, w, g, q, qt, q4, kv, sc, pr, mx, ot, o, oz, zs, rz, tb, xin, yin, ym, zin,
     acc, do, dz, dost, dos4, dsb, dkv, ci, fi, ri, rj, st,
     lsem, wsem,
-    agx_s, agx_r, agz_s, agz_r,
+    agx_s, agx_r, agz_s, agz_r, zx_s, zx_r,
     kv_s, kv_r, kf_s,
     zh_s, zh_r,
     a_s, a_r, x_s, x_r, y_s, y_r, m_s, m_r,
@@ -169,6 +169,23 @@
         for j in range(1, 4):
             keep(g.at[block(x), acols(a)], g.at[block(x), acols(a)], agx_s.at[j - 1, a], agx_r.at[j - 1, a], beside[j])
 
+    def zblock(pos):
+        return pl.ds(pl.multiple_of(64 + pos * PART, PART), PART)
+
+    def z_first():
+        last = NA - 1
+        here = g.at[zblock(x), acols(last)]
+        arrived(here, agz_r.at[x, last], zp, agz_s.at[0, last])
+        for j in (1, 3, 2):
+            keep(here, here, zx_s.at[j - 1], zx_r.at[j - 1], beside[j])
+
+    def ag_last():
+        last = NA - 1
+        for j in (1, 3, 2):
+            pos = (x + 4 - j) % 4
+            arrived(g.at[block(pos), acols(last)], agx_r.at[j - 1, last], core, agx_s.at[j - 1, last])
+            arrived(g.at[zblock(pos), acols(last)], zx_r.at[j - 1], core, zx_s.at[j - 1])
+
     def ag_part(a, j):
         pos = (x + 4 - j) % 4
         arrived(g.at[block(pos), acols(a)], agx_r.at[j - 1, a], core, agx_s.at[j - 1, a])
@@ -287,10 +304,11 @@
         )
 
     def attn_grad(a):
-        for pos in range(4):
-            arrived(
-                g.at[64 + pos * PART : 64 + (pos + 1) * PART, acols(a)], agz_r.at[pos, a], zp, agz_s.at[0, a]
-            )
+        if a == NA - 1:
+            ag_last()
+        else:
+            for pos in range(4):
+                arrived(g.at[zblock(pos), acols(a)], agz_r.at[pos, a], zp, agz_s.at[0, a])
         part = dot(g[:, acols(a)], w[:, acols(a)], ((1,), (1,)))
         acc[...] = part if a == 0 else acc[...] + part
 
@@ -395,11 +413,12 @@
 
         keep(st, fi, fi_s.at[0], fi_r.at[0], zhp)
 
-    for a in range(NA):
+    for a in (NA - 1, *range(NA - 1)):
         to_z(x, a, 0)
     scores(0)
     flip_step()
     key_step(2)
+    z_first()
     key_step(4)
     ag_step(0)
     ag_step(1)
@@ -409,7 +428,6 @@
     odd_step(0)
     odd_step(3)
     odd_step(2)
-    ag_step(2)
     peak = jnp.max(mx[...], axis=0, keepdims=True)
 
     def weigh(d, total):
@@ -431,13 +449,13 @@
     mine = o[orow(64 * zl, 64), :]
 
     oz[0:32, :] = o[orow(64 * (1 - zl), 32), :]
-    ag_step(3)
+    spread(0, 0)
+    ag_step(2)
+    give(0, 1)
     own(0)
-    spread(0, 0)
     own(1)
     own(2)
     own(3)
-    give(0, 1)
     arrived(oz.at[32:64, :], zh_r.at[0], zhp, zh_s.at[0])
     spread(1, 0)
     give(1, 1)
@@ -562,7 +580,7 @@
         pltpu.VMEM((2, ROWS, 2 * HEAD), BF16),
         pltpu.VMEM((ROWS, 2 * HEAD), BF16),
         dma((5,)), dma((NC,)),
-        dma((3, NA)), dma((3, NA)), dma((4, NA)), dma((4, NA)),
+        dma((3, NA)), dma((3, NA)), dma((4, NA)), dma((4, NA)), dma((3,)), dma((3,)),
         dma((5,)), dma((SLOTS + 1,)), dma((4,)),
         dma((2,)), dma((2,)),
         dma((2, NC)), dma((2, NC)), dma((4, NC)), dma((4, NC)),

time: 48.7 us -> 47 us (0.965)
  Pallas kernels: 47.9 us -> 46.1 us
    pallas_call x1, Pallas kernels: 46.1 us -> 44.3 us  [body(): pl.pallas_call(kernel, out_shape=shapes, in_specs=[hbm] * 6, out_specs=(v...]
where the time goes in v4:
time: 47 us; the launch traced here: 46.8 us
  Pallas kernels  46.1 us (98%)
  between operations  0.64 us (1%)
    pallas_call x1, Pallas kernels, body(): pl.pallas_call(kernel, out_shape=shapes, in_specs=[hbm] * 6, out_specs=(v...  44.3 us
    pallas_call x1, Pallas kernels, body(): pl.pallas_call(store, out_shape=shapes, in_specs=[vmem] * 4, out_specs=(h...  1.82 us

profile of v4, /device:TPU:1, one launch (start us, length us, event | category | flops | bytes accessed | tf_op | source)
XLA Modules:
  0.0 46.8 jit_solution(13266745699332334522)
XLA Ops:
  0.6 44.3 %shard_map.93 = (bf16[16,8192]{1,0:T(8,128)(2,1)}, bf16[128,512]{1,0:T(8,128)(2,1)}, bf16[128,128]{1,0:T(8,128)(2,1)}, bf16[128,128]{1,0:T(8,128)(2,1)}) custom-call(s32[12]{0:T(128)} %docs_hbm.1, bf16[128,512]{1,0:T(8,128)(2,1)} %q_hbm.1, bf16[128,128]{1,0:T(8,128)(2,1)} %k_hbm.1, bf16[128,128]{1,0:T(8,128)(2,1)} %v_hbm.1, bf16[512,8192]{1,0:T(8,128)(2,1)} %w_hbm.1, ...), custom_call_target="tpu_custom_call" | custom-call | tf_op jit(solution)/shard_map/pallas_call | solution.py:596
  45.0 1.8 %shard_map.94 = (bf16[16,8192]{1,0:T(8,128)(2,1)}, bf16[128,512]{1,0:T(8,128)(2,1)}, bf16[128,128]{1,0:T(8,128)(2,1)}, bf16[128,128]{1,0:T(8,128)(2,1)}) custom-call(bf16[16,8192]{1,0:T(8,128)(2,1)} %get-tuple-element.8.refs_0_, bf16[128,512]{1,0:T(8,128)(2,1)} %get-tuple-element.9.refs_1_, bf16[128,128]{1,0:T(8,128)(2,1)} %get-tuple-element.10.refs_2_, ...), custom_call_target="tpu_custom_call" | custom-call | tf_op jit(solution)/shard_map/pallas_call | solution.py:606

commit v5 on v4

--- a/solution.py
+++ b/solution.py
@@ -453,12 +453,12 @@
     ag_step(2)
     give(0, 1)
     own(0)
+    arrived(oz.at[32:64, :], zh_r.at[0], zhp, zh_s.at[0])
+    spread(1, 0)
+    give(1, 1)
     own(1)
     own(2)
     own(3)
-    arrived(oz.at[32:64, :], zh_r.at[0], zhp, zh_s.at[0])
-    spread(1, 0)
-    give(1, 1)
     attn_grad(0)
     attn_grad(1)
     attn_grad(2)

time: 47 us -> 48.5 us (1.032)
  Pallas kernels: 46.1 us -> 47.1 us
    pallas_call x1, Pallas kernels: 44.3 us -> 45.3 us  [body(): pl.pallas_call(kernel, out_shape=shapes, in_specs=[hbm] * 6, out_specs=(v...]
where the time goes in v5:
time: 48.5 us; the launch traced here: 47.8 us
  Pallas kernels  47.1 us (97%)
  between operations  0.64 us (1%)
    pallas_call x1, Pallas kernels, body(): pl.pallas_call(kernel, out_shape=shapes, in_specs=[hbm] * 6, out_specs=(v...  45.3 us
    pallas_call x1, Pallas kernels, body(): pl.pallas_call(store, out_shape=shapes, in_specs=[vmem] * 4, out_specs=(h...  1.82 us

profile of v5, /device:TPU:1, one launch (start us, length us, event | category | flops | bytes accessed | tf_op | source)
XLA Modules:
  0.0 47.8 jit_solution(13509444317789969334)
XLA Ops:
  0.6 45.3 %shard_map.93 = (bf16[16,8192]{1,0:T(8,128)(2,1)}, bf16[128,512]{1,0:T(8,128)(2,1)}, bf16[128,128]{1,0:T(8,128)(2,1)}, bf16[128,128]{1,0:T(8,128)(2,1)}) custom-call(s32[12]{0:T(128)} %docs_hbm.1, bf16[128,512]{1,0:T(8,128)(2,1)} %q_hbm.1, bf16[128,128]{1,0:T(8,128)(2,1)} %k_hbm.1, bf16[128,128]{1,0:T(8,128)(2,1)} %v_hbm.1, bf16[512,8192]{1,0:T(8,128)(2,1)} %w_hbm.1, ...), custom_call_target="tpu_custom_call" | custom-call | tf_op jit(solution)/shard_map/pallas_call | solution.py:596
  46.0 1.8 %shard_map.94 = (bf16[16,8192]{1,0:T(8,128)(2,1)}, bf16[128,512]{1,0:T(8,128)(2,1)}, bf16[128,128]{1,0:T(8,128)(2,1)}, bf16[128,128]{1,0:T(8,128)(2,1)}) custom-call(bf16[16,8192]{1,0:T(8,128)(2,1)} %get-tuple-element.8.refs_0_, bf16[128,512]{1,0:T(8,128)(2,1)} %get-tuple-element.9.refs_1_, bf16[128,128]{1,0:T(8,128)(2,1)} %get-tuple-element.10.refs_2_, ...), custom_call_target="tpu_custom_call" | custom-call | tf_op jit(solution)/shard_map/pallas_call | solution.py:606
